TPU v7x, 32 devices: a whole 2x2x4 slice. The times are simulated.
32 devices in a mesh: seq: 8 (over y, x, core), wa: 4 (over z).
Axes of the slice: x: 2, y: 2, z: 4, core: 2. Of those that a mesh axis runs over, the one named last changes fastest.
Arguments:
- hidden_in: bfloat16 [4096, 2048], P('seq', 'wa'), may hold values from -6 to 6
- request_spans: int32 [4, 2], replicated, may hold values from 0 to 4096, as said below
- owners: int32 [4], replicated, may hold values from 0 to 7, as said below
- mixer_gain: float32 [2048], replicated, may hold values from 0.1 to 1.9
- query_weight: bfloat16 [2048, 2048], P(None, 'wa'), may hold values from -0.125 to 0.125
- forget_weight: bfloat16 [2048, 2048], P(None, 'wa'), may hold values from -0.0625 to 0.0625
- input_weight: bfloat16 [2048, 2048], P(None, 'wa'), may hold values from -0.125 to 0.125
- gate_weight: bfloat16 [2048, 2048], P(None, 'wa'), may hold values from -0.125 to 0.125
- forget_bias: float32 [2048], P('wa')
- output_weight: bfloat16 [2048, 2048], P('wa'), may hold values from -0.125 to 0.125
- swiglu_gain: float32 [2048], replicated, may hold values from 0.1 to 1.9
- swiglu_gate: bfloat16 [2048, 3072], P(None, 'wa'), may hold values from -0.125 to 0.125
- swiglu_up: bfloat16 [2048, 3072], P(None, 'wa'), may hold values from -0.125 to 0.125
- swiglu_down: bfloat16 [3072, 2048], P('wa'), may hold values from -0.109375 to 0.109375
Outputs:
- hidden_out: bfloat16 [4096, 2048], P('seq', 'wa')
- handed_state: float32 [8, 16, 128, 128], P('seq', 'wa')
Inputs may be any that keep to these rules, and one draw needn't show every extreme that they name: Requests lie back to back in order: request_spans[0, 0] = 0, each request's end equals the next one's start, the last end is 4096, and every request holds at least 64 tokens. The owners are distinct indices along seq; the last request's owner is the index half of 8 minus one; the first request's owner is the index just before that of the device holding the first request's last token, counted round; the index 7 is always an owner.
All inputs are finite; a program needn't handle non-finite values.
Results may differ from a plain program's by a relative error of at most 0.009.
Values may be sent and summed in bfloat16 or wider, within the bound.
A program may use at most 128 MiB of HBM per device.

v0:
```python
import jax
import jax.numpy as jnp
from jax import lax
from jax.sharding import PartitionSpec as P

HEAD = 128
GROUP = 64
REQS = 4


EPS = 1e-06
HIGH = lax.Precision.HIGHEST


def entering(value, axis, join, neutral):
    count, mine = (lax.axis_size(axis), lax.axis_index(axis))
    pieces = jax.tree.map(lambda part: lax.all_gather(part, axis), value)
    so_far = jax.tree.map(
        lambda part, zero: jnp.full_like(part, 0) + jnp.asarray(zero, part.dtype), value, neutral
    )

    def hop(position, so_far):
        longer = join(so_far, jax.tree.map(lambda part: part[position], pieces))
        return jax.tree.map(lambda new, old: jnp.where(position < mine, new, old), longer, so_far)

    return lax.fori_loop(0, count - 1, hop, so_far)


def rms_rows(matrix, scaling):
    matrix = matrix.astype(jnp.float32)
    rescale = lax.rsqrt(jnp.mean(matrix * matrix, axis=-1, keepdims=True) + EPS)
    return (matrix * rescale * scaling).astype(jnp.bfloat16)


def project(matrix, weight):
    return jnp.dot(matrix, weight, preferred_element_type=jnp.float32)


def widen_rows(shard_part):
    return lax.all_gather(shard_part, "wa", axis=1, tiled=True)


def narrow_sum(partial_terms):
    return lax.psum_scatter(partial_terms, "wa", scatter_dimension=1, tiled=True)


def local(
    hidden_in,
    request_spans,
    owners,
    mixer_gain,
    query_weight,
    forget_weight,
    input_weight,
    gate_weight,
    forget_bias,
    output_weight,
    swiglu_gain,
    swiglu_gate,
    swiglu_up,
    swiglu_down,
):
    tok_rows = hidden_in.shape[0]
    head_count = query_weight.shape[1] // HEAD
    block_count = tok_rows // GROUP
    gathered = widen_rows(hidden_in)
    normed = rms_rows(gathered, mixer_gain)
    queries = jax.nn.silu(project(normed, query_weight))
    forget_logit = project(normed, forget_weight) + forget_bias
    log_decay = jax.nn.log_sigmoid(forget_logit)
    key_rows = jax.nn.sigmoid(-forget_logit)
    value_rows = project(normed, input_weight)
    gate_logit = project(normed, gate_weight)
    first_row = lax.axis_index("seq") * tok_rows
    position = first_row + jnp.arange(tok_rows, dtype=jnp.int32)
    start_rows = request_spans[:, 0]
    end_rows = request_spans[:, 1]
    is_start = jnp.any(position[:, None] == start_rows[None, :], axis=1)
    segment = jnp.sum((start_rows[None, :] <= position[:, None]).astype(jnp.int32), axis=1) - 1
    shape_four = (block_count, GROUP, head_count, HEAD)
    query_parts = queries.reshape(shape_four)
    key_parts = key_rows.reshape(shape_four)
    value_parts = value_rows.reshape(shape_four)
    segment_parts = segment.reshape(block_count, GROUP)
    keep_mask = (1.0 - is_start.astype(jnp.float32)).reshape(block_count, GROUP)
    cum_decay = jnp.cumsum(log_decay.reshape(shape_four), axis=1)
    surviving = jnp.cumprod(keep_mask, axis=1)
    query_tilde = query_parts * jnp.exp(cum_decay)
    key_tilde = key_parts * jnp.exp(-cum_decay)
    offsets = jnp.arange(GROUP, dtype=jnp.int32)
    causal = offsets[:, None] >= offsets[None, :]
    same_doc = causal[None] & (segment_parts[:, :, None] == segment_parts[:, None, :])
    scores = jnp.einsum("nihc,njhc->nhij", query_tilde, key_tilde, precision=HIGH)
    scores = jnp.where(same_doc[:, None], scores, 0.0)
    inner_out = jnp.einsum("nhij,njhd->nihd", scores, value_parts, precision=HIGH)
    tail_mask = (segment_parts == segment_parts[:, -1:]).astype(jnp.float32)
    last_decay = jnp.exp(cum_decay[:, -1])
    fresh = last_decay[..., None] * jnp.einsum(
        "njhc,njhd->nhcd", key_tilde * tail_mask[:, :, None, None], value_parts, precision=HIGH
    )
    shrink = surviving[:, -1][:, None, None] * last_decay

    def advance(carried, blocked):
        running, product = carried
        shrink_part, fresh_part = blocked
        return (
            (shrink_part[..., None] * running + fresh_part, product * shrink_part),
            (running, product),
        )

    initial = (
        jnp.zeros((head_count, HEAD, HEAD), jnp.float32),
        jnp.ones((head_count, HEAD), jnp.float32),
    )
    (local_state, device_decay), (start_state, start_decay) = lax.scan(
        advance, initial, (shrink, fresh)
    )

    def combine(earlier, follower):
        return (earlier[0] * follower[0], follower[0][..., None] * earlier[1] + follower[1])

    identity = (jnp.ones_like(device_decay), jnp.zeros_like(local_state))
    incoming = entering((device_decay, local_state), "seq", combine, identity)[1]
    block_state = start_state + start_decay[..., None] * incoming[None]
    carried_out = jnp.einsum("nihc,nhcd->nihd", query_tilde, block_state, precision=HIGH)
    mixer_out = (inner_out + surviving[:, :, None, None] * carried_out).reshape(
        tok_rows, head_count, HEAD
    )
    rescale = lax.rsqrt(jnp.mean(mixer_out * mixer_out, axis=-1, keepdims=True) + EPS)
    gate_heads = jax.nn.silu(gate_logit.reshape(tok_rows, head_count, HEAD))
    mixed_rows = (
        (mixer_out * rescale * gate_heads).reshape(tok_rows, head_count * HEAD).astype(jnp.bfloat16)
    )
    collected = []
    for request in range(REQS):
        local_end = end_rows[request] - 1 - first_row
        inside = (local_end >= 0) & (local_end < tok_rows)
        end_row = jnp.clip(local_end, 0, tok_rows - 1)
        block_index = end_row // GROUP
        within = end_row % GROUP
        decay_block = lax.dynamic_index_in_dim(cum_decay, block_index, 0, keepdims=False)
        key_block = lax.dynamic_index_in_dim(key_tilde, block_index, 0, keepdims=False)
        value_block = lax.dynamic_index_in_dim(value_parts, block_index, 0, keepdims=False)
        segment_block = lax.dynamic_index_in_dim(segment_parts, block_index, 0, keepdims=False)
        alive_block = lax.dynamic_index_in_dim(surviving, block_index, 0, keepdims=False)
        state_block = lax.dynamic_index_in_dim(block_state, block_index, 0, keepdims=False)
        decay_end = lax.dynamic_index_in_dim(decay_block, within, 0, keepdims=False)
        segment_end = lax.dynamic_index_in_dim(segment_block, within, 0, keepdims=False)
        alive_end = lax.dynamic_index_in_dim(alive_block, within, 0, keepdims=False)
        upto_mask = ((offsets <= within) & (segment_block == segment_end)).astype(jnp.float32)
        partial_end = jnp.einsum(
            "jhc,jhd->hcd", key_block * upto_mask[:, None, None], value_block, precision=HIGH
        )
        end_state = jnp.exp(decay_end)[..., None] * (alive_end * state_block + partial_end)
        collected.append(jnp.where(inside, end_state, 0.0))
    end_states = jnp.stack(collected)
    summed_states = lax.psum(end_states.astype(jnp.bfloat16), "seq").astype(jnp.float32)
    owned_mask = (owners == lax.axis_index("seq")).astype(jnp.float32)
    handed_state = jnp.einsum("r,rhcd->hcd", owned_mask, summed_states, precision=HIGH)[None]
    partial_terms = project(mixed_rows, output_weight)
    residual = (hidden_in.astype(jnp.float32) + narrow_sum(partial_terms)).astype(jnp.bfloat16)
    widened = widen_rows(residual)
    normed_ffn = rms_rows(widened, swiglu_gain)
    hidden = (
        jax.nn.silu(project(normed_ffn, swiglu_gate)) * project(normed_ffn, swiglu_up)
    ).astype(jnp.bfloat16)
    hidden_out = (residual.astype(jnp.float32) + narrow_sum(project(hidden, swiglu_down))).astype(
        jnp.bfloat16
    )
    return (hidden_out, handed_state)


def solution(mesh):
    in_specs = (
        P("seq", "wa"),
        P(),
        P(),
        P(),
        P(None, "wa"),
        P(None, "wa"),
        P(None, "wa"),
        P(None, "wa"),
        P("wa"),
        P("wa", None),
        P(),
        P(None, "wa"),
        P(None, "wa"),
        P("wa", None),
    )
    out_specs = (P("seq", "wa"), P("seq", "wa", None, None))
    return jax.shard_map(local, mesh=mesh, in_specs=in_specs, out_specs=out_specs, check_vma=False)
```

profile of v0, /device:TPU:6, one launch (start us, length us, event | category | flops | bytes accessed | tf_op | source)
XLA Modules:
  0.0 434.7 jit_solution(5393584060082983810)
XLA Ops:
  9.9 46.8 %all-gather.7.cloned.1.call-done = bf16[512,2048]{1,0:T(8,128)(2,1)} async-done(((bf16[512,512]{1,0:T(8,128)(2,1)}), bf16[512,2048]{1,0:T(8,128)(2,1)}) %all-gather.7.cloned.1.call-update) | async-done | bytes 2097168 | tf_op jit(solution)/shard_map/all_gather | solution.py:40
  56.7 2.2 fusion.1
  59.0 4.9 %add_divide_fusion = (f32[512,512]{1,0:T(8,128)}, f32[512,512]{1,0:T(8,128)}) fusion(f32[512]{0:T(512)S(1)} %copy-done.15, bf16[2048,512]{1,0:T(8,128)(2,1)} %param.23, bf16[512,2048]{1,0:T(8,128)(2,1)S(1)} %copy-done.8, f32[2048]{0:T(1024)S(1)} %copy-done.13, f32[512]{0:T(512)S(1)} %add_rsqrt_fusion.1), kind=kOutput, calls=%fused_computation.60 | convolution fusion | flops 1080819712 | bytes 6303744 | tf_op jit(solution)/shard_map/dot_general | solution.py:36
  63.9 2.5 reshape.259
  66.5 2.6 reshape.260
  69.0 4.7 %divide_multiply_fusion = f32[512,512]{1,0:T(8,128)} fusion(bf16[2048,512]{1,0:T(8,128)(2,1)} %param.22, bf16[512,2048]{1,0:T(8,128)(2,1)} %all-gather.7.cloned.1.call-done, f32[2048]{0:T(1024)S(1)} %copy-done.13, f32[512]{0:T(512)S(1)} %add_rsqrt_fusion.1), kind=kOutput, calls=%fused_computation.61 | convolution fusion | flops 1078984704 | bytes 5253120 | tf_op jit(solution)/shard_map/dot_general | solution.py:36
  73.7 2.5 reshape.258
  76.2 4.9 %broadcast_multiply_fusion = (f32[8,64,4,128]{3,0,1,2:T(8,128)}, f32[8,64,4,128]{3,0,1,2:T(8,128)}, f32[8,64,4,128]{3,0,1,2:T(8,128)}, f32[8,64,4,128]{3,0,1,2:T(8,128)S(1)}) fusion(f32[8,64]{0,1:T(8,128)S(1)} %copy.108, f32[8,64,4,128]{3,2,1,0:T(4,128)} %reshape.260, f32[8,64,4,128]{3,2,1,0:T(4,128)} %reshape.258, f32[8,64,4,128]{3,2,1,0:T(4,128)} %reshape.259), kind=kOutput, calls=%fused_computation.70 | output fusion | flops 17563648 | bytes 7342080 | tf_op jit(solution)/shard_map/jit(cumsum)/reduce_window_sum | solution.py:86
  82.1 2.3 fusion.80
  84.4 2.5 reshape.257
  87.7 6.8 %convolution_multiply_fusion = f32[8,4,128,128]{3,2,1,0:T(8,128)} fusion(f32[8,64,4,128]{3,0,1,2:T(8,128)} %get-tuple-element.249, f32[8,4,128]{2,1,0:T(4,128)S(1)} %copy.107, f32[8,64,4,128]{3,2,1,0:T(4,128)} %reshape.257), kind=kOutput, calls=%fused_computation.20 | convolution fusion | flops 403177472 | bytes 4210688 | tf_op jit(solution)/shard_map/njhc,njhd->nhcd/dot_general | solution.py:98
  94.5 15.2 %while.31 = (s32[]{:T(128)}, f32[4,128,128]{2,1,0:T(8,128)S(1)}, f32[4,128]{1,0:T(4,128)S(1)}, f32[8,4,128,128]{3,2,1,0:T(8,128)}, f32[8,4,128]{2,1,0:T(4,128)S(...) while((s32[]{:T(128)}, f32[4,128,128]{2,1,0:T(8,128)S(1)}, ...), condition=%wide.region_6.7_spmd.clone, body=%wide.region_5.6_spmd.clone.sunk | while | flops 263683 | bytes 1327734 | solution.py:115
  95.2 1.1 bitcast_add_fusion.3
  97.1 1.1 bitcast_add_fusion.3
  110.7 8.0 %all-gather.2 = f32[8,4,128]{2,1,0:T(4,128)S(1)} all-gather(f32[1,4,128]{2,1,0:T(4,128)S(1)} %bitcast.143), channel_id=2, replica_groups=mesh['seq'=8,'wa'=4] {'seq'}, dimensions={0}, use_global_device_ids=true | all-gather | bytes 18432 | tf_op jit(solution)/shard_map/all_gather | solution.py:17
  118.7 4.5 %convolution_select_fusion = f32[8,4,64,64]{3,2,1,0:T(8,128)} fusion(f32[8,64,4,128]{3,0,1,2:T(8,128)} %get-tuple-element.250, f32[8,64,4,128]{3,0,1,2:T(8,128)} %get-tuple-element.263, pred[8,64,64]{2,1,0:T(8,128)(4,1)S(1)} %compare_and_fusion), kind=kOutput, calls=%fused_computation.25 | convolution fusion | flops 201457664 | bytes 2654208 | tf_op jit(solution)/shard_map/nihc,njhc->nhij/dot_general | solution.py:93
  123.2 13.1 %all-gather.11.cloned.1.call-done = f32[32,128,128]{2,1,0:T(8,128)} async-done(((f32[4,128,128]{2,1,0:T(8,128)}), f32[32,128,128]{2,1,0:T(8,128)}) %all-gather.11.cloned.1.call-update) | async-done | bytes 2097168 | tf_op jit(solution)/shard_map/all_gather | solution.py:17
  136.3 8.3 %while.32 = (s32[]{:T(128)}, f32[4,128,128]{2,1,0:T(8,128)S(1)}, s32[]{:T(128)}, f32[8,4,128]{2,1,0:T(4,128)S(1)}, f32[8,4,128,128]{3,2,1,0:T(8,128)}, /*index=5*/s32[]{:T(128)}, s32[]{:T(128)}) while((s32[]{:T(128)}, f32[4,128,128]{2,1,0:T(8,128)S(1)}, s32[]{:T(128)}, f32[8,4,128]{2,1,0:T(4,128)S(1)}, ...), condition=%wide.region_8.9_spmd.clone, body=%wide.region_7.8_spmd.clone.sunk | while | flops 262148 | bytes 792681 | solution.py:26
  136.3 1.1 fusion.102
  137.5 1.1 fusion.102
  138.7 1.1 fusion.102
  139.9 1.1 fusion.102
  141.1 1.1 fusion.102
  142.3 1.1 fusion.102
  143.5 1.1 fusion.102
  144.7 2.0 multiply_add_fusion
  146.7 2.0 convolution_multiply_fusion.1
  149.0 2.2 multiply_reduce_fusion
  151.3 2.9 copy.113
  154.3 1.7 mul.291
  155.9 8.0 %fusion.40 = f32[512,2048]{1,0:T(8,128)} fusion(bf16[512,2048]{1,0:T(8,128)(2,1)} %param.27, f32[64,8,4,128]{3,2,1,0:T(4,128)} %bitcast.133, f32[64,8,4,128]{3,2,1,0:T(4,128)} %bitcast.135, bf16[2048,512]{1,0:T(8,128)(2,1)} %param.25, bf16[512,2048]{1,0:T(8,128)(2,1)} %all-gather.7.cloned.1.call-done, f32[2048]{0:T(1024)S(1)} %copy-done.13, ...), kind=kOutput, calls=%fused_computation.68 | convolution fusion | flops 2153512960 | bytes 12593152 | tf_op jit(solution)/shard_map/dot_general | solution.py:36
  164.0 77.8 %reduce-scatter.3.cloned.1.call-done = f32[512,512]{1,0:T(8,128)} async-done(((f32[512,2048]{1,0:T(8,128)}), f32[512,512]{1,0:T(8,128)}) %reduce-scatter.3.cloned.1.call-update) | async-done | bytes 1048592 | tf_op jit(solution)/shard_map/reduce_scatter | solution.py:44
  241.8 2.3 add_convert_fusion.1
  249.1 2.6 fusion.71
  252.6 3.2 constant_dynamic-slice_fusion.15
  255.8 1.1 constant_dynamic-slice_fusion.13
  256.9 1.3 fusion.23
  258.3 1.3 fusion.22
  259.6 1.3 fusion.21
  261.0 1.4 fusion.20
  263.3 27.4 %all-gather.9.cloned.1.call-done = bf16[512,2048]{1,0:T(8,128)(2,1)} async-done(((bf16[512,512]{1,0:T(8,128)(2,1)}), bf16[512,2048]{1,0:T(8,128)(2,1)}) %all-gather.9.cloned.1.call-update) | async-done | bytes 2097168 | tf_op jit(solution)/shard_map/all_gather | solution.py:40
  290.7 2.2 fusion.4
  292.9 5.0 %fusion.38 = f32[512,768]{1,0:T(8,128)} fusion(bf16[2048,768]{1,0:T(8,128)(2,1)} %param.29, bf16[512,2048]{1,0:T(8,128)(2,1)S(1)} %copy-done.7, f32[2048]{0:T(1024)S(1)} %copy-done.14, f32[512]{0:T(512)S(1)} %add_rsqrt_fusion), kind=kOutput, calls=%fused_computation.67 | convolution fusion | flops 1614807040 | bytes 6825984 | tf_op jit(solution)/shard_map/dot_general | solution.py:36
  297.9 9.0 %fusion.35 = f32[512,2048]{1,0:T(8,128)} fusion(bf16[768,2048]{1,0:T(8,128)(2,1)S(1)} %copy-done, f32[512,768]{1,0:T(8,128)} %fusion.38, bf16[2048,768]{1,0:T(8,128)(2,1)} %param.30, bf16[512,2048]{1,0:T(8,128)(2,1)} %all-gather.9.cloned.1.call-done, f32[2048]{0:T(1024)S(1)} %copy-done.14, f32[512]{0:T(512)S(1)} %add_rsqrt_fusion), kind=kOutput, calls=%fused_computation.66 | convolution fusion | flops 3227779072 | bytes 14166016 | tf_op jit(solution)/shard_map/dot_general | solution.py:36
  306.9 38.7 %all-reduce.2.cloned.1.call-done = bf16[4,4,128,128]{3,2,1,0:T(8,128)(2,1)} async-done(((bf16[4,4,128,128]{3,2,1,0:T(8,128)(2,1)}), bf16[4,4,128,128]{3,2,1,0:T(8,128)(2,1)}) %all-reduce.2.cloned.1.call-update) | async-done | bytes 524304 | tf_op jit(solution)/shard_map/psum | solution.py:157
  345.6 2.2 fusion.43
  347.8 77.7 %reduce-scatter.5.cloned.1.call-done = f32[512,512]{1,0:T(8,128)} async-done(((f32[512,2048]{1,0:T(8,128)}), f32[512,512]{1,0:T(8,128)}) %reduce-scatter.5.cloned.1.call-update) | async-done | bytes 1048592 | tf_op jit(solution)/shard_map/reduce_scatter | solution.py:44
  425.5 2.3 add_convert_fusion
  (123 shorter events, 22.7 us)
Async XLA Ops:
  7.2 290.7 %copy-start = (bf16[768,2048]{1,0:T(8,128)(2,1)S(1)}, bf16[768,2048]{1,0:T(8,128)(2,1)}, u32[]{:S(2)}) copy-start(bf16[768,2048]{1,0:T(8,128)(2,1)} %param.31) | copy-start | bytes 9437188
  7.2 51.8 %copy-start.13 = (f32[2048]{0:T(1024)S(1)}, f32[2048]{0:T(1024)}, u32[]{:S(2)}) copy-start(f32[2048]{0:T(1024)} %param.21) | copy-start | bytes 24580
  7.2 51.8 %copy-start.15 = (f32[512]{0:T(512)S(1)}, f32[512]{0:T(512)}, u32[]{:S(2)}) copy-start(f32[512]{0:T(512)} %param.26) | copy-start | bytes 6148
  7.2 49.5 %all-gather.7.cloned.1.call-start = ((), (), s32[]{:S(2)}) async-start(), calls=%async_computation.2 | async-start | bytes 2621440 | tf_op jit(solution)/shard_map/all_gather | solution.py:40
  7.9 128.4 %all-gather.11.cloned.1.call-start = ((), (), s32[]{:S(2)}) async-start(), calls=%async_computation.7 | async-start | bytes 2359296 | tf_op jit(solution)/shard_map/all_gather | solution.py:17
  56.7 2.3 copy-start.8
  76.2 5.9 %copy-start.9 = (bf16[512,2048]{1,0:T(8,128)(2,1)S(1)}, bf16[512,2048]{1,0:T(8,128)(2,1)}, u32[]{:S(2)}) copy-start(bf16[512,2048]{1,0:T(8,128)(2,1)} %all-gather.7.cloned.1.call-done) | copy-start | bytes 6291460
  76.2 5.9 %copy-start.12 = (bf16[2048,512]{1,0:T(8,128)(2,1)S(1)}, bf16[2048,512]{1,0:T(8,128)(2,1)}, u32[]{:S(2)}) copy-start(bf16[2048,512]{1,0:T(8,128)(2,1)} %param.24) | copy-start | bytes 6291460
  81.1 0.9 copy-start.10
  109.7 0.7 copy-start.1
  110.5 131.3 %reduce-scatter.3.cloned.1.call-start = ((), (), s32[]{:S(2)}) async-start(), calls=%async_computation.3 | async-start | bytes 5242880 | tf_op jit(solution)/shard_map/reduce_scatter | solution.py:44
  144.6 2.1 copy-start.5
  146.7 2.1 copy-start.2
  146.7 2.1 copy-start.4
  146.7 2.3 copy-start.6
  163.9 80.5 %copy-start.11 = (s32[4,2]{0,1:T(2,128)S(1)}, s32[4,2]{0,1:T(2,128)}, u32[]{:S(2)}) copy-start(s32[4,2]{0,1:T(2,128)} %param.19) | copy-start | bytes 100
  163.9 126.8 %all-gather.9.cloned.1.call-start = ((), (), s32[]{:S(2)}) async-start(), calls=%async_computation.4 | async-start | bytes 2621440 | tf_op jit(solution)/shard_map/all_gather | solution.py:40
  244.1 101.5 %all-reduce.2.cloned.1.call-start = ((), (), s32[]{:S(2)}) async-start(), calls=%async_computation.6 | async-start | bytes 1048576 | tf_op jit(solution)/shard_map/psum | solution.py:157
  247.8 9.1 %copy-start.3 = (f32[8,4,128,128]{3,2,1,0:T(8,128)S(1)}, f32[8,4,128,128]{3,2,1,0:T(8,128)}, u32[]{:S(2)}) copy-start(f32[8,4,128,128]{3,2,1,0:T(8,128)} %copy-done.2) | copy-start | bytes 6291460
  260.9 32.0 %copy-start.14 = (f32[2048]{0:T(1024)S(1)}, f32[2048]{0:T(1024)}, u32[]{:S(2)}) copy-start(f32[2048]{0:T(1024)} %param.28) | copy-start | bytes 24580
  263.3 162.2 %reduce-scatter.5.cloned.1.call-start = ((), (), s32[]{:S(2)}) async-start(), calls=%async_computation.5 | async-start | bytes 5242880 | tf_op jit(solution)/shard_map/reduce_scatter | solution.py:44
  290.7 2.2 copy-start.7
  306.9 38.7 %copy-start.16 = (s32[4]{0:T(128)S(1)}, s32[4]{0:T(128)}, u32[]{:S(2)}) copy-start(s32[4]{0:T(128)} %param.20) | copy-start | bytes 52
Sparse Core Ops, SparseCore 0:
  9.6 47.0 all-gather.6
  110.6 25.6 all-gather.10
  164.0 77.6 reduce-scatter.2
  244.2 46.4 all-gather.8
  293.9 51.5 all-reduce.1
  347.7 77.7 reduce-scatter.4
where the time goes:
time: 438 us; the launch traced here: 435 us
  waiting for transfers between devices  282 us (64%)
  matrix products  57 us (13%)
  other arithmetic  43.9 us (10%)
  local copies, waits for them, and re-layouts  25.5 us (6%)
  between operations  17.2 us (4%)
  blocking collectives  7.98 us (2%)
    reduce_scatter x2, waiting for transfers between devices, narrow_sum(): lax.psum_scatter(partial_terms, 'wa', scatter_dimension=1, tiled=True)  155 us
    all_gather x2, waiting for transfers between devices, widen_rows(): return lax.all_gather(shard_part, 'wa', axis=1, tiled=True)  74.2 us
    psum x1, waiting for transfers between devices, local(): lax.psum(end_states.astype(jnp.bfloat16), 'seq').astype(jnp.float32)  38.7 us
    dot_general x6, matrix products, project(): return jnp.dot(matrix, weight, preferred_element_type=jnp.float32)  33.8 us
    all_gather x1, waiting for transfers between devices, entering(): pieces = jax.tree.map(lambda part: lax.all_gather(part, axis), value)  13.1 us
    add x8, other arithmetic, advance(): shrink_part[..., None] * running + fresh_part  8.93 us
  transfers between devices with their start and end apart: 6, of which 6 were waited for; matrix products, arithmetic and copies ran while one was open for 9% of the time, Pallas kernels for 0%

commit v1 on v0

v1 whole, which is shorter than its diff:
```python
import jax
import jax.numpy as jnp
from jax import lax
from jax.experimental import pallas as pl
from jax.experimental.pallas import tpu as pltpu
from jax.sharding import PartitionSpec as P

HEAD = 128
GROUP = 64
REQS = 4
CHUNKS = 4
EPS = 1e-06
HIGH = lax.Precision.HIGHEST
MESH = pl.DeviceIdType.MESH
BF = jnp.bfloat16
F32 = jnp.float32
VMEM_BYTES = 58 * 1024 * 1024


def dot(a, b, contract=(1, 0), precision=None):
    return lax.dot_general(
        a, b, (((contract[0],), (contract[1],)), ((), ())), precision=precision,
        preferred_element_type=F32,
    )


def inside(index, count):
    return (index >= 0) & (index < count)


def greet_wa(me, count, barrier):
    for sgn in (1, -1):
        @pl.when(inside(me + sgn, count))
        def _():
            pl.semaphore_signal(barrier, inc=1, device_id={"wa": me + sgn}, device_id_type=MESH)


class Gather:
    def __init__(self, buf, send_sem, recv_sem, me, count, rows):
        self.buf, self.send_sem, self.recv_sem = buf, send_sem, recv_sem
        self.me, self.count, self.rows = me, count, rows

    def copy(self, src, c, sgn, target):
        ref = self.buf.at[src, pl.ds(c * self.rows, self.rows)]
        return pltpu.make_async_remote_copy(
            src_ref=ref, dst_ref=ref,
            send_sem=self.send_sem.at[(sgn + 1) // 2, src, c],
            recv_sem=self.recv_sem.at[src, c],
            device_id={"wa": target}, device_id_type=MESH,
        )

    def own(self, c):
        for sgn in (1, -1):
            @pl.when(inside(self.me + sgn, self.count))
            def _():
                self.copy(self.me, c, sgn, self.me + sgn).start()

    def arrive(self, c):
        for k in range(1, self.count):
            for sgn in (1, -1):
                src = self.me - sgn * k

                @pl.when(inside(src, self.count))
                def _():
                    self.copy(src, c, sgn, self.me - sgn).wait_recv()

                    @pl.when(inside(self.me + sgn, self.count))
                    def _():
                        self.copy(src, c, sgn, self.me + sgn).start()

    def drain(self):
        for c in range(CHUNKS):
            for k in range(self.count):
                for sgn in (1, -1):
                    src = self.me - sgn * k

                    @pl.when(inside(src, self.count) & inside(self.me + sgn, self.count))
                    def _():
                        self.copy(src, c, sgn, self.me + sgn).wait_send()


class Scatter:
    def __init__(self, part, out, came, send_sem, recv_sem, me, count, rows):
        self.part, self.out, self.came = part, out, came
        self.send_sem, self.recv_sem = send_sem, recv_sem
        self.me, self.count, self.rows = me, count, rows
        first = jnp.where(2 * me < count, 1, -1)
        self.ways = (first, -first)

    def copy(self, w, c, sgn, target):
        span = pl.ds(c * self.rows, self.rows)
        way = (sgn + 1) // 2
        return pltpu.make_async_remote_copy(
            src_ref=self.out.at[w, span], dst_ref=self.came.at[way, w, span],
            send_sem=self.send_sem.at[w, c], recv_sem=self.recv_sem.at[way, w, c],
            device_id={"wa": target}, device_id_type=MESH,
        )

    def hop(self, c):
        span = pl.ds(c * self.rows, self.rows)
        me, count = self.me, self.count
        for sgn in self.ways:
            way = (sgn + 1) // 2
            for k in range(count - 1, 0, -1):
                w = me + sgn * k

                @pl.when(inside(w, count))
                def _():
                    @pl.when(inside(me - sgn, count))
                    def _():
                        self.copy(w, c, sgn, me - sgn).wait_recv()
                        self.out[w, span] = (
                            self.part[w, span] + self.came[way, w, span].astype(F32)
                        ).astype(BF)

                    @pl.when(jnp.logical_not(inside(me - sgn, count)))
                    def _():
                        self.out[w, span] = self.part[w, span].astype(BF)

                    self.copy(w, c, sgn, me + sgn).start()

    def total(self, c):
        span = pl.ds(c * self.rows, self.rows)
        me, count = self.me, self.count
        for sgn in self.ways:
            way = (sgn + 1) // 2

            @pl.when(inside(me - sgn, count))
            def _():
                self.copy(me, c, sgn, me - sgn).wait_recv()
                self.part[me, span] = self.part[me, span] + self.came[way, me, span].astype(F32)
        return self.part[me, span]

    def drain(self):
        for c in range(CHUNKS):
            for sgn in (1, -1):
                for k in range(1, self.count):
                    w = self.me + sgn * k

                    @pl.when(inside(w, self.count))
                    def _():
                        self.copy(w, c, sgn, self.me + sgn).wait_send()


def rms_chunk(buf, count, c, rows, gain):
    span = pl.ds(c * rows, rows)
    pieces = [buf[s, span].astype(F32) for s in range(count)]
    width = pieces[0].shape[1]
    square = sum(jnp.sum(piece * piece, axis=1, keepdims=True) for piece in pieces)
    rescale = lax.rsqrt(square / (width * count) + EPS)
    return jnp.concatenate(
        [
            (piece * rescale * gain[:, s * width:(s + 1) * width]).astype(BF)
            for s, piece in enumerate(pieces)
        ],
        axis=1,
    )


def silu(v):
    return v / (1.0 + jnp.exp(-v))


def enter_kernel(
    hidden, gain, bias, wq, wf, wi, wg,
    q_out, ld_out, k_out, v_out, g_out,
    buf, vq, vf, vi, vg, w_sem, own_sem, send_sem, recv_sem,
):
    me, count = lax.axis_index("wa"), lax.axis_size("wa")
    rows = hidden.shape[0] // CHUNKS
    loads = [
        pltpu.make_async_copy(src, dst, w_sem.at[i])
        for i, (src, dst) in enumerate(((wq, vq), (wf, vf), (wi, vi), (wg, vg)))
    ]
    mine = pltpu.make_async_copy(hidden, buf.at[me], own_sem)
    mine.start()
    barrier = pltpu.get_barrier_semaphore()
    greet_wa(me, count, barrier)
    mine.wait()
    near = inside(me - 1, count).astype(jnp.int32) + inside(me + 1, count).astype(jnp.int32)
    pl.semaphore_wait(barrier, near)
    ag = Gather(buf, send_sem, recv_sem, me, count, rows)
    ag.own(0)
    ag.own(1)
    for load in loads:
        load.start()
    for c in range(CHUNKS):
        ag.arrive(c)
        if c + 2 < CHUNKS:
            ag.own(c + 2)
        if c == 0:
            for load in loads:
                load.wait()
        span = pl.ds(c * rows, rows)
        normed = rms_chunk(buf, count, c, rows, gain[...])
        q_out[span] = silu(dot(normed, vq[...]))
        logit = dot(normed, vf[...]) + bias[...]
        ld_out[span] = jnp.minimum(logit, 0.0) - jnp.log1p(jnp.exp(-jnp.abs(logit)))
        k_out[span] = 1.0 / (1.0 + jnp.exp(logit))
        v_out[span] = dot(normed, vi[...]).astype(BF)
        g_out[span] = silu(dot(normed, vg[...]))
    ag.drain()


def block_kernel(
    spans, first_ref, q, ld, k, v,
    out, qp, state_out, decay_out, ends, end_decay,
    state, decay,
):
    heads = q.shape[1] // HEAD
    blocks = q.shape[0] // GROUP
    state[...] = jnp.zeros_like(state)
    decay[...] = jnp.ones_like(decay)
    ends[...] = jnp.zeros_like(ends)
    end_decay[...] = jnp.zeros_like(end_decay)
    below = lax.broadcasted_iota(jnp.int32, (GROUP, GROUP), 0)
    across = lax.broadcasted_iota(jnp.int32, (GROUP, GROUP), 1)
    causal = below >= across
    lower = causal.astype(F32)
    column = lax.broadcasted_iota(jnp.int32, (GROUP, 1), 0)
    line = lax.broadcasted_iota(jnp.int32, (1, GROUP), 1)

    def began(position):
        return sum((spans[r, 0] <= position).astype(jnp.int32) for r in range(REQS))

    def body(n, carry):
        rows = pl.ds(pl.multiple_of(n * GROUP, GROUP), GROUP)
        base = first_ref[0] + n * GROUP
        cum = dot(lower, ld[rows], precision=HIGH)
        qt = q[rows] * jnp.exp(cum)
        kt = k[rows] * jnp.exp(-cum)
        vb = v[rows]
        seg = began(base + column)
        mask = causal & (seg == began(base + line))
        prev, last = began(base - 1), began(base + GROUP - 1)
        surviving = (seg == prev).astype(F32)
        tail = (seg == last).astype(F32)
        alive = (last == prev).astype(F32)
        for r in range(REQS):
            within = spans[r, 1] - 1 - base

            @pl.when((within >= 0) & (within < GROUP))
            def _():
                upto = ((column <= within) & (seg == r + 1)).astype(F32)
                alive_end = (prev == r + 1).astype(F32)
                at_end = jnp.exp(
                    jnp.sum(jnp.where(column == within, cum, 0.0), axis=0, keepdims=True)
                )
                for h in range(heads):
                    hs = slice(h * HEAD, (h + 1) * HEAD)
                    partial = dot(vb[:, hs], (kt[:, hs] * upto).astype(BF), (0, 0))
                    ends[r, h] = at_end[:, hs] * (alive_end * state[h] + partial)
                    end_decay[r, h:h + 1] = at_end[:, hs] * alive_end * decay[h:h + 1]

        for h in range(heads):
            hs = slice(h * HEAD, (h + 1) * HEAD)
            qh, vh = qt[:, hs].astype(BF), vb[:, hs]
            scores = dot(qh, kt[:, hs].astype(BF), (1, 1))
            scores = jnp.where(mask, scores, 0.0).astype(BF)
            held, shrunk = state[h], decay[h:h + 1]
            out[rows, hs] = dot(scores, vh) + surviving * dot(qh, held.astype(BF), (1, 1))
            qp[rows, hs] = (qt[:, hs] * surviving * shrunk).astype(BF)
            fresh = dot(vh, (kt[:, hs] * tail).astype(BF), (0, 0))
            full = jnp.exp(cum[GROUP - 1:GROUP, hs])
            state[h] = full * (alive * held + fresh)
            decay[h:h + 1] = shrunk * (full * alive)
        return carry

    lax.fori_loop(0, blocks, body, 0)
    state_out[...] = state[...].astype(BF)
    decay_out[...] = decay[...]


def leave_kernel(
    owners, hidden, out_local, qp, g, state, decay, ends, end_decay, gain, wo, wgate, wup, wdown,
    y_out, handed_out,
    vo, vgate, vup, vdown, part1, part2, out1, out2, came1, came2, buf,
    states, decays, incoming, end_mine, end_out, end_came,
    w_sem, rs1_send, rs1_recv, rs2_send, rs2_recv, ag_send, ag_recv,
    st_send, st_recv, de_send, de_recv, en_send, en_recv,
):
    me, count = lax.axis_index("wa"), lax.axis_size("wa")
    place, places = lax.axis_index("seq"), lax.axis_size("seq")
    rows = hidden.shape[0] // CHUNKS
    width = hidden.shape[1]
    heads = width // HEAD
    loads = [
        pltpu.make_async_copy(src, dst, w_sem.at[i])
        for i, (src, dst) in enumerate(((wo, vo), (wgate, vgate), (wup, vup), (wdown, vdown)))
    ]
    barrier = pltpu.get_barrier_semaphore()
    greet_wa(me, count, barrier)

    def others(act):
        def step(j, carry):
            act(lax.rem(place + j, places))
            return carry
        lax.fori_loop(1, places, step, 0)

    others(lambda peer: pl.semaphore_signal(
        barrier, inc=1, device_id={"seq": peer}, device_id_type=MESH))
    near = inside(me - 1, count).astype(jnp.int32) + inside(me + 1, count).astype(jnp.int32)
    pl.semaphore_wait(barrier, near + (places - 1))

    def state_copy(source, peer, send):
        return pltpu.make_async_remote_copy(
            src_ref=state, dst_ref=states.at[source], send_sem=st_send.at[send],
            recv_sem=st_recv.at[source], device_id={"seq": peer}, device_id_type=MESH)

    def decay_copy(source, peer, send):
        return pltpu.make_async_remote_copy(
            src_ref=decay, dst_ref=decays.at[source], send_sem=de_send.at[send],
            recv_sem=de_recv.at[source], device_id={"seq": peer}, device_id_type=MESH)

    def end_copy(source, peer, send):
        return pltpu.make_async_remote_copy(
            src_ref=end_out.at[send], dst_ref=end_came.at[source], send_sem=en_send.at[send],
            recv_sem=en_recv.at[source], device_id={"seq": peer}, device_id_type=MESH)

    def later(act):
        def step(peer, carry):
            act(peer)
            return carry
        lax.fori_loop(place + 1, places, step, 0)

    def push(peer):
        state_copy(place, peer, peer).start()
        decay_copy(place, peer, peer).start()

    later(push)
    for load in loads:
        load.start()
    incoming[...] = jnp.zeros_like(incoming)

    def join(p, carry):
        state_copy(p, p, p).wait_recv()
        decay_copy(p, p, p).wait_recv()
        for h in range(heads):
            incoming[h] = incoming[h] * decays[p, h:h + 1] + states[p, h].astype(F32)
        return carry

    lax.fori_loop(0, place, join, 0)
    loads[0].wait()

    rs1 = Scatter(part1, out1, came1, rs1_send, rs1_recv, me, count, rows)
    rs2 = Scatter(part2, out2, came2, rs2_send, rs2_recv, me, count, rows)
    ag = Gather(buf, ag_send, ag_recv, me, count, rows)

    def mix(c):
        span = pl.ds(c * rows, rows)
        mixed = []
        for h in range(heads):
            hs = slice(h * HEAD, (h + 1) * HEAD)
            o = out_local[span, hs] + dot(qp[span, hs], incoming[h].astype(BF), (1, 1))
            rescale = lax.rsqrt(jnp.mean(o * o, axis=1, keepdims=True) + EPS)
            mixed.append((o * rescale * g[span, hs]).astype(BF))
        mixed = jnp.concatenate(mixed, axis=1)
        for w in range(count):
            part1[w, span] = dot(mixed, vo[:, w * width:(w + 1) * width])

    def settle(c):
        span = pl.ds(c * rows, rows)
        rs1.hop(c)
        buf[me, span] = (hidden[span].astype(F32) + rs1.total(c)).astype(BF)
        ag.own(c)

    def feed(c):
        span = pl.ds(c * rows, rows)
        ag.arrive(c)
        normed = rms_chunk(buf, count, c, rows, gain[...])
        units = (silu(dot(normed, vgate[...])) * dot(normed, vup[...])).astype(BF)
        for w in range(count):
            part2[w, span] = dot(units, vdown[:, w * width:(w + 1) * width])

    def finish(c):
        span = pl.ds(c * rows, rows)
        rs2.hop(c)
        y_out[span] = (buf[me, span].astype(F32) + rs2.total(c)).astype(BF)

    def hand_over():
        for r in range(REQS):
            for h in range(heads):
                end_mine[r, h] = ends[r, h] + end_decay[r, h:h + 1] * incoming[h]

        def fill(peer, carry):
            picks = [(owners[r] == peer).astype(F32) for r in range(REQS)]
            for h in range(heads):
                end_out[peer, h] = sum(picks[r] * end_mine[r, h] for r in range(REQS)).astype(BF)
            return carry

        lax.fori_loop(0, places, fill, 0)
        others(lambda peer: end_copy(place, peer, peer).start())

    mix(0)
    mix(1)
    settle(0)
    mix(2)
    settle(1)
    mix(3)
    hand_over()
    settle(2)
    for load in loads[1:]:
        load.wait()
    feed(0)
    settle(3)
    feed(1)
    finish(0)
    feed(2)
    finish(1)
    feed(3)
    finish(2)
    finish(3)

    others(lambda peer: end_copy(peer, peer, peer).wait_recv())
    end_came[place] = end_out[place]
    for h in range(heads):
        def gather_end(p, total):
            return total + end_came[p, h].astype(F32)
        handed_out[0, h] = lax.fori_loop(
            0, places, gather_end, jnp.zeros((HEAD, HEAD), F32)).T
    others(lambda peer: end_copy(place, peer, peer).wait_send())

    def sent(peer):
        state_copy(place, peer, peer).wait_send()
        decay_copy(place, peer, peer).wait_send()

    later(sent)
    rs1.drain()
    rs2.drain()
    ag.drain()


def local(
    hidden_in, request_spans, owners, mixer_gain, query_weight, forget_weight, input_weight,
    gate_weight, forget_bias, output_weight, swiglu_gain, swiglu_gate, swiglu_up, swiglu_down,
):
    count, places = lax.axis_size("wa"), lax.axis_size("seq")
    tok, width = hidden_in.shape
    heads = width // HEAD
    depth = query_weight.shape[0]
    ff = swiglu_gate.shape[1]
    vmem = pl.BlockSpec(memory_space=pltpu.VMEM)
    smem = pl.BlockSpec(memory_space=pltpu.SMEM)
    hbm = pl.BlockSpec(memory_space=pl.ANY)
    DMA = pltpu.SemaphoreType.DMA

    q, ld, k, v, g = pl.pallas_call(
        enter_kernel,
        out_shape=[jax.ShapeDtypeStruct((tok, width), t) for t in (F32, F32, F32, BF, F32)],
        in_specs=[vmem] * 3 + [hbm] * 4,
        out_specs=[vmem] * 5,
        scratch_shapes=[pltpu.VMEM((count, tok, width), BF)]
        + [pltpu.VMEM((depth, width), BF)] * 4
        + [DMA((4,)), DMA, DMA((2, count, CHUNKS)), DMA((count, CHUNKS))],
        compiler_params=pltpu.CompilerParams(
            collective_id=0, has_side_effects=True, vmem_limit_bytes=VMEM_BYTES),
        name="enter",
    )(
        hidden_in, mixer_gain[None], forget_bias[None],
        query_weight, forget_weight, input_weight, gate_weight,
    )

    first = (lax.axis_index("seq") * tok).astype(jnp.int32)[None]
    out_local, qp, state, decay, ends, end_decay = pl.pallas_call(
        block_kernel,
        out_shape=[
            jax.ShapeDtypeStruct((tok, width), F32),
            jax.ShapeDtypeStruct((tok, width), BF),
            jax.ShapeDtypeStruct((heads, HEAD, HEAD), BF),
            jax.ShapeDtypeStruct((heads, HEAD), F32),
            jax.ShapeDtypeStruct((REQS, heads, HEAD, HEAD), F32),
            jax.ShapeDtypeStruct((REQS, heads, HEAD), F32),
        ],
        in_specs=[smem, smem] + [vmem] * 4,
        out_specs=[vmem] * 6,
        scratch_shapes=[pltpu.VMEM((heads, HEAD, HEAD), F32), pltpu.VMEM((heads, HEAD), F32)],
        compiler_params=pltpu.CompilerParams(vmem_limit_bytes=VMEM_BYTES),
        name="blocks",
    )(request_spans, first, q, ld, k, v)

    y, handed = pl.pallas_call(
        leave_kernel,
        out_shape=[
            jax.ShapeDtypeStruct((tok, width), BF),
            jax.ShapeDtypeStruct((1, heads, HEAD, HEAD), F32),
        ],
        in_specs=[smem] + [vmem] * 9 + [hbm] * 4,
        out_specs=[vmem] * 2,
        scratch_shapes=[
            pltpu.VMEM((width, depth), BF),
            pltpu.VMEM((depth, ff), BF),
            pltpu.VMEM((depth, ff), BF),
            pltpu.VMEM((ff, depth), BF),
            pltpu.VMEM((count, tok, width), F32),
            pltpu.VMEM((count, tok, width), F32),
            pltpu.VMEM((count, tok, width), BF),
            pltpu.VMEM((count, tok, width), BF),
            pltpu.VMEM((2, count, tok, width), BF),
            pltpu.VMEM((2, count, tok, width), BF),
            pltpu.VMEM((count, tok, width), BF),
            pltpu.VMEM((places, heads, HEAD, HEAD), BF),
            pltpu.VMEM((places, heads, HEAD), F32),
            pltpu.VMEM((heads, HEAD, HEAD), F32),
            pltpu.VMEM((REQS, heads, HEAD, HEAD), F32),
            pltpu.VMEM((places, heads, HEAD, HEAD), BF),
            pltpu.VMEM((places, heads, HEAD, HEAD), BF),
            DMA((4,)),
            DMA((count, CHUNKS)), DMA((2, count, CHUNKS)),
            DMA((count, CHUNKS)), DMA((2, count, CHUNKS)),
            DMA((2, count, CHUNKS)), DMA((count, CHUNKS)),
            DMA((places,)), DMA((places,)), DMA((places,)), DMA((places,)),
            DMA((places,)), DMA((places,)),
        ],
        compiler_params=pltpu.CompilerParams(
            collective_id=1, has_side_effects=True, vmem_limit_bytes=VMEM_BYTES),
        name="leave",
    )(
        owners, hidden_in, out_local, qp, g, state, decay, ends, end_decay,
        swiglu_gain[None], output_weight, swiglu_gate, swiglu_up, swiglu_down,
    )
    return y, handed


def solution(mesh):
    in_specs = (
        P("seq", "wa"), P(), P(), P(), P(None, "wa"), P(None, "wa"), P(None, "wa"),
        P(None, "wa"), P("wa"), P("wa", None), P(), P(None, "wa"), P(None, "wa"), P("wa", None),
    )
    out_specs = (P("seq", "wa"), P("seq", "wa", None, None))
    return jax.shard_map(local, mesh=mesh, in_specs=in_specs, out_specs=out_specs, check_vma=False)
```

time: 438 us -> 226 us (0.52)
  waiting for transfers between devices: 282 us -> 0 us
  Pallas kernels: 0 us -> 221 us
  matrix products: 57 us -> 0 us
  other arithmetic: 43.9 us -> 0 us
  local copies, waits for them, and re-layouts: 25.5 us -> 4.86 us
  between operations: 17.2 us -> 0.65 us
  blocking collectives: 7.98 us -> 0 us
    pallas_call x0 -> x3, Pallas kernels: none -> 221 us  [the longest x1 164 us: local(): pl.pallas_call(leave_kernel, out_shape=[jax.ShapeDtypeStruct((tok, width)...]
    reduce_scatter x2 -> x0, waiting for transfers between devices: 155 us -> none  [narrow_sum(): lax.psum_scatter(partial_terms, 'wa', scatter_dimension=1, tiled=True)]
    all_gather x3 -> x0, waiting for transfers between devices: 87.3 us -> none  [the longest x2 74.2 us: widen_rows(): return lax.all_gather(shard_part, 'wa', axis=1, tiled=True)]
    dot_general x15 -> x0, matrix products: 57 us -> none  [the longest x6 33.8 us: project(): return jnp.dot(matrix, weight, preferred_element_type=jnp.float32)]
    psum x1 -> x0, waiting for transfers between devices: 38.7 us -> none  [local(): lax.psum(end_states.astype(jnp.bfloat16), 'seq').astype(jnp.float32)]
    add x10 -> x0, other arithmetic: 11 us -> none  [the longest x8 8.93 us: advance(): shrink_part[..., None] * running + fresh_part]
    reshape x4 -> x0, local copies, waits for them, and re-layouts: 10.2 us -> none  [the longest x1 2.56 us: local(): key_parts = key_rows.reshape(shape_four)]
    select_n x7 -> x0, other arithmetic: 8.04 us -> none  [hop(): jnp.where(position < mine, new, old)]
  transfers between devices with their start and end apart: 6 -> 0, of which waited for: 6 -> 0; matrix products, arithmetic and copies ran while one was open for 9% -> 0% of each run, Pallas kernels for 0% -> 0%
where the time goes in v1:
time: 226 us
  Pallas kernels  221 us (98%)
  local copies, waits for them, and re-layouts  4.86 us (2%)
    pallas_call x1, Pallas kernels, local(): pl.pallas_call(leave_kernel, out_shape=[jax.ShapeDtypeStruct((tok, width)...  164 us
    pallas_call x1, Pallas kernels, local(): pl.pallas_call(enter_kernel, out_shape=[jax.ShapeDtypeStruct((tok, width)...  44 us
    pallas_call x1, Pallas kernels, local(): pl.pallas_call(block_kernel, out_shape=[jax.ShapeDtypeStruct((tok, width)...  12.3 us
    unnamed x3, local copies, waits for them, and re-layouts  4.86 us

profile of v1, /device:TPU:6, one launch (start us, length us, event | category | flops | bytes accessed | tf_op | source)
XLA Modules:
  0.0 226.1 jit_solution(17176090067924938665)
XLA Ops:
  0.6 1.3 copy.16.spans
  2.0 44.0 %enter.1 = (f32[512,512]{1,0:T(8,128)}, f32[512,512]{1,0:T(8,128)}, f32[512,512]{1,0:T(8,128)}, bf16[512,512]{1,0:T(8,128)(2,1)}, f32[512,512]{1,0:T(8,128)}) custom-call(bf16[512,512]{1,0:T(8,128)(2,1)} %hidden.3, f32[1,2048]{1,0:T(1,128)} %bitcast.5, f32[1,512]{1,0:T(1,128)} %bitcast.6, bf16[2048,512]{1,0:T(8,128)(2,1)} %wq.1, bf16[2048,512]{1,0:T(8,128)(2,1)} %wf.1, ...), custom_call_target="tpu_custom_call" | custom-call | tf_op jit(solution)/shard_map/enter/pallas_call | solution.py:447
  46.0 12.3 %blocks.1 = (f32[512,512]{1,0:T(8,128)}, bf16[512,512]{1,0:T(8,128)(2,1)}, bf16[4,128,128]{2,1,0:T(8,128)(2,1)}, f32[4,128]{1,0:T(4,128)}, f32[4,4,128,128]{3,2,1,0:T(8,128)}, /*index=5*/f32[4,4,128]{2,1,0:T(4,128)}) custom-call(s32[4,2]{1,0:T(4,128)} %copy.16.spans, s32[1]{0:T(128)} %bitcast.first_ref, f32[512,512]{1,0:T(8,128)} %get-tuple-element.13.q, ...), custom_call_target="tpu_custom_call" | custom-call | tf_op jit(solution)/shard_map/blocks/pallas_call | solution.py:464
  58.3 164.3 %leave.1 = (bf16[512,512]{1,0:T(8,128)(2,1)}, f32[1,4,128,128]{3,2,1,0:T(8,128)}) custom-call(s32[4]{0:T(128)} %owners.1, bf16[512,512]{1,0:T(8,128)(2,1)} %hidden.3, f32[512,512]{1,0:T(8,128)} %get-tuple-element.17.out_local, bf16[512,512]{1,0:T(8,128)(2,1)} %get-tuple-element.18.qp, f32[512,512]{1,0:T(8,128)} %get-tuple-element.19.g, ...), custom_call_target="tpu_custom_call" | custom-call | tf_op jit(solution)/shard_map/leave/pallas_call | solution.py:481
  222.5 1.9 copy.19
  224.4 1.7 copy.20

commit v2 on v1

--- a/solution.py
+++ b/solution.py
@@ -96,27 +96,25 @@
             device_id={"wa": target}, device_id_type=MESH,
         )
 
-    def hop(self, c):
+    def hop(self, c, relay):
         span = pl.ds(c * self.rows, self.rows)
         me, count = self.me, self.count
         for sgn in self.ways:
             way = (sgn + 1) // 2
+            fed = inside(me - sgn, count)
+            turn = fed if relay else jnp.logical_not(fed)
             for k in range(count - 1, 0, -1):
                 w = me + sgn * k
 
-                @pl.when(inside(w, count))
+                @pl.when(inside(w, count) & turn)
                 def _():
-                    @pl.when(inside(me - sgn, count))
-                    def _():
+                    if relay:
                         self.copy(w, c, sgn, me - sgn).wait_recv()
                         self.out[w, span] = (
                             self.part[w, span] + self.came[way, w, span].astype(F32)
                         ).astype(BF)
-
-                    @pl.when(jnp.logical_not(inside(me - sgn, count)))
-                    def _():
+                    else:
                         self.out[w, span] = self.part[w, span].astype(BF)
-
                     self.copy(w, c, sgn, me + sgn).start()
 
     def total(self, c):
@@ -360,7 +358,6 @@
 
     def settle(c):
         span = pl.ds(c * rows, rows)
-        rs1.hop(c)
         buf[me, span] = (hidden[span].astype(F32) + rs1.total(c)).astype(BF)
         ag.own(c)
 
@@ -374,7 +371,6 @@
 
     def finish(c):
         span = pl.ds(c * rows, rows)
-        rs2.hop(c)
         y_out[span] = (buf[me, span].astype(F32) + rs2.total(c)).astype(BF)
 
     def hand_over():
@@ -392,23 +388,39 @@
         others(lambda peer: end_copy(place, peer, peer).start())
 
     mix(0)
+    rs1.hop(0, False)
     mix(1)
+    rs1.hop(1, False)
+    rs1.hop(0, True)
+    mix(2)
+    rs1.hop(2, False)
     settle(0)
-    mix(2)
+    rs1.hop(1, True)
+    mix(3)
+    rs1.hop(3, False)
     settle(1)
-    mix(3)
+    rs1.hop(2, True)
     hand_over()
-    settle(2)
     for load in loads[1:]:
         load.wait()
     feed(0)
+    rs2.hop(0, False)
+    settle(2)
+    rs1.hop(3, True)
+    feed(1)
+    rs2.hop(1, False)
     settle(3)
-    feed(1)
+    rs2.hop(0, True)
+    feed(2)
+    rs2.hop(2, False)
     finish(0)
-    feed(2)
+    rs2.hop(1, True)
+    feed(3)
+    rs2.hop(3, False)
     finish(1)
-    feed(3)
+    rs2.hop(2, True)
     finish(2)
+    rs2.hop(3, True)
     finish(3)
 
     others(lambda peer: end_copy(peer, peer, peer).wait_recv())

time: 226 us -> 178 us (0.79)
  Pallas kernels: 221 us -> 172 us
    pallas_call x1, Pallas kernels: 164 us -> 116 us  [local(): pl.pallas_call(leave_kernel, out_shape=[jax.ShapeDtypeStruct((tok, width)...]
where the time goes in v2:
time: 178 us
  Pallas kernels  172 us (97%)
  local copies, waits for them, and re-layouts  4.86 us (3%)
    pallas_call x1, Pallas kernels, local(): pl.pallas_call(leave_kernel, out_shape=[jax.ShapeDtypeStruct((tok, width)...  116 us
    pallas_call x1, Pallas kernels, local(): pl.pallas_call(enter_kernel, out_shape=[jax.ShapeDtypeStruct((tok, width)...  44 us
    pallas_call x1, Pallas kernels, local(): pl.pallas_call(block_kernel, out_shape=[jax.ShapeDtypeStruct((tok, width)...  11.9 us
    unnamed x3, local copies, waits for them, and re-layouts  4.86 us

profile of v2, /device:TPU:6, one launch (start us, length us, event | category | flops | bytes accessed | tf_op | source)
XLA Modules:
  0.0 177.8 jit_solution(14230820730419810659)
XLA Ops:
  0.6 1.3 copy.16.spans
  2.0 44.0 %enter.1 = (f32[512,512]{1,0:T(8,128)}, f32[512,512]{1,0:T(8,128)}, f32[512,512]{1,0:T(8,128)}, bf16[512,512]{1,0:T(8,128)(2,1)}, f32[512,512]{1,0:T(8,128)}) custom-call(bf16[512,512]{1,0:T(8,128)(2,1)} %hidden.3, f32[1,2048]{1,0:T(1,128)} %bitcast.5, f32[1,512]{1,0:T(1,128)} %bitcast.6, bf16[2048,512]{1,0:T(8,128)(2,1)} %wq.1, bf16[2048,512]{1,0:T(8,128)(2,1)} %wf.1, ...), custom_call_target="tpu_custom_call" | custom-call | tf_op jit(solution)/shard_map/enter/pallas_call | solution.py:459
  46.0 11.9 %blocks.1 = (f32[512,512]{1,0:T(8,128)}, bf16[512,512]{1,0:T(8,128)(2,1)}, bf16[4,128,128]{2,1,0:T(8,128)(2,1)}, f32[4,128]{1,0:T(4,128)}, f32[4,4,128,128]{3,2,1,0:T(8,128)}, /*index=5*/f32[4,4,128]{2,1,0:T(4,128)}) custom-call(s32[4,2]{1,0:T(4,128)} %copy.16.spans, s32[1]{0:T(128)} %bitcast.first_ref, f32[512,512]{1,0:T(8,128)} %get-tuple-element.13.q, ...), custom_call_target="tpu_custom_call" | custom-call | tf_op jit(solution)/shard_map/blocks/pallas_call | solution.py:476
  57.8 116.5 %leave.1 = (bf16[512,512]{1,0:T(8,128)(2,1)}, f32[1,4,128,128]{3,2,1,0:T(8,128)}) custom-call(s32[4]{0:T(128)} %owners.1, bf16[512,512]{1,0:T(8,128)(2,1)} %hidden.3, f32[512,512]{1,0:T(8,128)} %get-tuple-element.17.out_local, bf16[512,512]{1,0:T(8,128)(2,1)} %get-tuple-element.18.qp, f32[512,512]{1,0:T(8,128)} %get-tuple-element.19.g, ...), custom_call_target="tpu_custom_call" | custom-call | tf_op jit(solution)/shard_map/leave/pallas_call | solution.py:493
  174.3 1.9 %copy.19 = bf16[512,512]{1,0:T(8,128)(2,1)} copy(bf16[512,512]{1,0:T(8,128)(2,1)} %get-tuple-element.26) | data formatting | bytes 1048576
  176.2 1.7 copy.20

commit v3 on v2

--- a/solution.py
+++ b/solution.py
@@ -103,6 +103,8 @@
             way = (sgn + 1) // 2
             fed = inside(me - sgn, count)
             turn = fed if relay else jnp.logical_not(fed)
+            if c > 0 and not relay:
+                self.sent(c - 1, sgn, turn)
             for k in range(count - 1, 0, -1):
                 w = me + sgn * k
 
@@ -129,15 +131,20 @@
                 self.part[me, span] = self.part[me, span] + self.came[way, me, span].astype(F32)
         return self.part[me, span]
 
+    def sent(self, c, sgn, turn):
+        for k in range(1, self.count):
+            w = self.me + sgn * k
+
+            @pl.when(inside(w, self.count) & turn)
+            def _():
+                self.copy(w, c, sgn, self.me + sgn).wait_send()
+
     def drain(self):
-        for c in range(CHUNKS):
-            for sgn in (1, -1):
-                for k in range(1, self.count):
-                    w = self.me + sgn * k
-
-                    @pl.when(inside(w, self.count))
-                    def _():
-                        self.copy(w, c, sgn, self.me + sgn).wait_send()
+        for sgn in (1, -1):
+            fed = inside(self.me - sgn, self.count)
+            for c in range(CHUNKS):
+                self.sent(c, sgn, fed)
+            self.sent(CHUNKS - 1, sgn, jnp.logical_not(fed))
 
 
 def rms_chunk(buf, count, c, rows, gain):

time: 178 us -> 176 us (0.989)
  no operation moved by 1% of the time
where the time goes in v3:
time: 176 us
  Pallas kernels  171 us (97%)
  local copies, waits for them, and re-layouts  4.86 us (3%)
    pallas_call x1, Pallas kernels, local(): pl.pallas_call(leave_kernel, out_shape=[jax.ShapeDtypeStruct((tok, width)...  115 us
    pallas_call x1, Pallas kernels, local(): pl.pallas_call(enter_kernel, out_shape=[jax.ShapeDtypeStruct((tok, width)...  44 us
    pallas_call x1, Pallas kernels, local(): pl.pallas_call(block_kernel, out_shape=[jax.ShapeDtypeStruct((tok, width)...  11.9 us
    unnamed x3, local copies, waits for them, and re-layouts  4.86 us

profile of v3, /device:TPU:6, one launch (start us, length us, event | category | flops | bytes accessed | tf_op | source)
XLA Modules:
  0.0 176.2 jit_solution(3935052427134208834)
XLA Ops:
  0.6 1.3 copy.16.spans
  2.0 44.0 %enter.1 = (f32[512,512]{1,0:T(8,128)}, f32[512,512]{1,0:T(8,128)}, f32[512,512]{1,0:T(8,128)}, bf16[512,512]{1,0:T(8,128)(2,1)}, f32[512,512]{1,0:T(8,128)}) custom-call(bf16[512,512]{1,0:T(8,128)(2,1)} %hidden.3, f32[1,2048]{1,0:T(1,128)} %bitcast.5, f32[1,512]{1,0:T(1,128)} %bitcast.6, bf16[2048,512]{1,0:T(8,128)(2,1)} %wq.1, bf16[2048,512]{1,0:T(8,128)(2,1)} %wf.1, ...), custom_call_target="tpu_custom_call" | custom-call | tf_op jit(solution)/shard_map/enter/pallas_call | solution.py:466
  46.0 11.9 %blocks.1 = (f32[512,512]{1,0:T(8,128)}, bf16[512,512]{1,0:T(8,128)(2,1)}, bf16[4,128,128]{2,1,0:T(8,128)(2,1)}, f32[4,128]{1,0:T(4,128)}, f32[4,4,128,128]{3,2,1,0:T(8,128)}, /*index=5*/f32[4,4,128]{2,1,0:T(4,128)}) custom-call(s32[4,2]{1,0:T(4,128)} %copy.16.spans, s32[1]{0:T(128)} %bitcast.first_ref, f32[512,512]{1,0:T(8,128)} %get-tuple-element.13.q, ...), custom_call_target="tpu_custom_call" | custom-call | tf_op jit(solution)/shard_map/blocks/pallas_call | solution.py:483
  57.8 114.8 %leave.1 = (bf16[512,512]{1,0:T(8,128)(2,1)}, f32[1,4,128,128]{3,2,1,0:T(8,128)}) custom-call(s32[4]{0:T(128)} %owners.1, bf16[512,512]{1,0:T(8,128)(2,1)} %hidden.3, f32[512,512]{1,0:T(8,128)} %get-tuple-element.17.out_local, bf16[512,512]{1,0:T(8,128)(2,1)} %get-tuple-element.18.qp, f32[512,512]{1,0:T(8,128)} %get-tuple-element.19.g, ...), custom_call_target="tpu_custom_call" | custom-call | tf_op jit(solution)/shard_map/leave/pallas_call | solution.py:500
  172.7 1.9 %copy.19 = bf16[512,512]{1,0:T(8,128)(2,1)} copy(bf16[512,512]{1,0:T(8,128)(2,1)} %get-tuple-element.26) | data formatting | bytes 1048576
  174.6 1.7 copy.20
